TPU v7x, 512 devices: a whole 4x4x16 slice. The times are simulated.
512 devices in a mesh: row: 32 (over y_hi, z), col: 16 (over y_lo, x, core).
Axes of the slice: x: 4, y: 4 (y_hi: 2, y_lo: 2; y = y_hi * 2 + y_lo), z: 16, core: 2. Of those that a mesh axis runs over, the one named last changes fastest.
Arguments:
- pair_rep: bfloat16 [512, 512, 128], P('row', 'col'), may hold values from -6 to 6
- input_gain: float32 [128], replicated, may hold values from 0.5 to 1.5
- input_bias: float32 [128], replicated, may hold values from -3 to 3
- proj_weight: bfloat16 [128, 512], replicated, may hold values from -0.5 to 0.5
- proj_bias: float32 [512], replicated, may hold values from -3 to 3
- norm_gain: float32 [128], replicated, may hold values from 0.5 to 1.5
- norm_bias: float32 [128], replicated, may hold values from -3 to 3
- out_weight: bfloat16 [128, 128], replicated, may hold values from -0.5 to 0.5
- out_bias: float32 [128], replicated, may hold values from -3 to 3
- gate_weight: bfloat16 [128, 128], replicated, may hold values from -0.5 to 0.5
- gate_bias: float32 [128], replicated, may hold values from -3 to 3
Outputs:
- update: bfloat16 [512, 512, 128], P('row', 'col')
All inputs are finite; a program needn't handle non-finite values.
Results may differ from a plain program's by a relative error of at most 0.0051.
Values may be sent and summed in bfloat16 or wider, within the bound.
A program may use at most 64 MiB of HBM per device.

v0:
```python
import jax
import jax.numpy as jnp
from jax import lax
from jax.sharding import PartitionSpec as P


def from_root(value, axis, root):
    mine = lax.axis_index(axis) == root
    return lax.psum(jnp.where(mine, value, jnp.zeros_like(value)), axis)


def layer_norm(values, gain, bias):
    mean = jnp.mean(values, axis=-1, keepdims=True)
    centred = values - mean
    var = jnp.mean(centred * centred, axis=-1, keepdims=True)
    return centred * jax.lax.rsqrt(var + 1e-05) * gain + bias


def normalize(pair_block, gain, bias):
    return layer_norm(pair_block.astype(jnp.float32), gain, bias).astype(jnp.bfloat16)


def gated_edge(normed, weight, bias, first):
    hidden = weight.shape[1] // 4
    shape = normed.shape
    cols = weight[:, first * hidden : (first + 2) * hidden]
    both = jnp.dot(normed.reshape(-1, shape[2]), cols, preferred_element_type=jnp.float32)
    both = both + bias[first * hidden : (first + 2) * hidden]
    edge = jax.nn.sigmoid(both[:, :hidden]) * both[:, hidden:]
    return edge.astype(jnp.bfloat16).reshape(shape[0], shape[1], hidden)


def per_device(
    pair_rep,
    input_gain,
    input_bias,
    proj_weight,
    proj_bias,
    norm_gain,
    norm_bias,
    out_weight,
    out_bias,
    gate_weight,
    gate_bias,
):
    hidden = norm_gain.shape[0]
    rows_here, cols_here, chans = pair_rep.shape
    groups = lax.axis_size("row") // lax.axis_size("col")
    owner_base = lax.axis_index("col") * groups
    normed = normalize(pair_rep, input_gain, input_bias)
    left_tile = gated_edge(normed, proj_weight, proj_bias, 0)
    right_tile = gated_edge(normed, proj_weight, proj_bias, 2)
    left_panel, right_rows = (
        lax.all_gather(left_tile, "col", axis=1, tiled=True),
        lax.all_gather(right_tile, "col", axis=1, tiled=True),
    )
    owned = [from_root(right_rows, "row", owner_base + member) for member in range(groups)]
    right_panel = jnp.concatenate(owned, axis=0)
    joined = jnp.einsum("ikh,jkh->ijh", left_panel, right_panel, preferred_element_type=jnp.float32)
    joined_norm = layer_norm(joined, norm_gain, norm_bias).astype(jnp.bfloat16).reshape(-1, hidden)
    flat = normed.reshape(-1, chans)
    gate = jax.nn.sigmoid(
        jnp.dot(flat, gate_weight, preferred_element_type=jnp.float32) + gate_bias
    )
    value = jnp.dot(joined_norm, out_weight, preferred_element_type=jnp.float32) + out_bias
    return (gate * value).astype(jnp.bfloat16).reshape(rows_here, cols_here, chans)


def solution(mesh):
    return jax.shard_map(
        per_device,
        mesh=mesh,
        in_specs=(P("row", "col", None), P(), P(), P(), P(), P(), P(), P(), P(), P(), P()),
        out_specs=P("row", "col", None),
        check_vma=False,
    )
```

profile of v0, /device:TPU:2, one launch (start us, length us, event | category | flops | bytes accessed | tf_op | source)
XLA Modules:
  0.0 433.6 jit_solution(869743203584507180)
XLA Ops:
  6.5 0.0 copy-start
  6.5 0.0 copy-start.1
  6.5 0.0 all-gather.3.cloned.1.call-start
  6.5 1.1 convert_reduce_fusion
  7.6 1.2 fusion.12
  8.8 0.8 fusion.27
  9.6 1.1 fusion.15
  10.7 1.1 convolution_add_fusion.1
  11.8 0.1 fusion.20
  11.9 0.7 copy.23
  12.5 0.0 all-gather.3.cloned.1.call-update
  12.6 0.0 all-gather.5.cloned.1.call-start
  12.6 0.0 copy-done.1
  12.6 0.2 convolution_add_fusion
  12.8 0.1 fusion.16
  12.9 0.7 copy.26
  13.6 0.0 all-gather.5.cloned.1.call-update
  13.7 0.0 all-reduce.3.cloned.1.call-start
  13.7 44.7 %all-gather.3.cloned.1.call-done = bf16[16,512,128]{2,0,1:T(8,128)(2,1)} async-done(((bf16[16,32,128]{2,0,1:T(8,128)(2,1)}), bf16[16,512,128]{2,0,1:T(8,128)(2,1)}) %all-gather.3.cloned.1.call-update) | async-done | bytes 2097168 | tf_op jit(solution)/shard_map/all_gather | solution.py:55
  58.4 3.9 copy.24
  62.3 2.3 broadcast_select_fusion.1
  64.6 0.0 copy-start.6
  64.6 0.0 all-reduce.3.cloned.1.call-update
  64.6 0.0 copy-done
  64.7 0.6 copy-done.6
  65.3 0.2 fusion.8
  65.5 36.9 %all-gather.5.cloned.1.call-done = bf16[16,512,128]{2,0,1:T(8,128)(2,1)} async-done(((bf16[16,32,128]{2,0,1:T(8,128)(2,1)}), bf16[16,512,128]{2,0,1:T(8,128)(2,1)}) %all-gather.5.cloned.1.call-update) | async-done | bytes 2097168 | tf_op jit(solution)/shard_map/all_gather | solution.py:54
  102.3 3.9 copy.27
  106.3 315.4 %all-reduce.3.cloned.1.call-done = (bf16[16,512,128]{1,0,2:T(8,128)(2,1)}, bf16[16,512,128]{1,0,2:T(8,128)(2,1)}) async-done(((bf16[16,512,128]{1,0,2:T(8,128)(2,1)}, bf16[16,512,128]{1,0,2:T(8,128)(2,1)}), (bf16[16,512,128]{1,0,2:T(8,128)(2,1)}, bf16[16,512,128]{1,0,2:T(8,128)(2,1)})) %all-reduce.3.cloned.1.call-update) | async-done | bytes 4194320 | tf_op jit(solution)/shard_map/psum | solution.py:9
  421.6 0.0 copy-start.3
  421.6 0.0 copy-start.4
  421.6 3.4 fusion
  425.1 0.0 copy-start.2
  425.1 0.0 copy-start.5
  425.1 0.4 copy.28
  425.5 0.1 bitcast_reduce_fusion
  425.7 0.3 multiply_reduce_fusion
  425.9 0.0 copy-done.3
  425.9 0.0 copy-done.4
  426.0 0.2 add_convert_fusion
  426.2 0.0 copy-done.2
  426.2 0.0 copy-done.5
  426.2 0.8 fusion.9
  (4 shorter events, 0.0 us)
Async XLA Ops:
  6.5 58.1 %copy-start = (bf16[128,128]{1,0:T(8,128)(2,1)S(1)}, bf16[128,128]{1,0:T(8,128)(2,1)}, u32[]{:S(2)}) copy-start(bf16[128,128]{1,0:T(8,128)(2,1)} %param.20) | copy-start | bytes 98308
  6.5 6.1 %copy-start.1 = (bf16[128,512]{1,0:T(8,128)(2,1)S(1)}, bf16[128,512]{1,0:T(8,128)(2,1)}, u32[]{:S(2)}) copy-start(bf16[128,512]{1,0:T(8,128)(2,1)} %param.14) | copy-start | bytes 393220
  6.5 51.8 %all-gather.3.cloned.1.call-start = ((), (), s32[]{:S(2)}) async-start(), calls=%async_computation | async-start | bytes 2228224 | tf_op jit(solution)/shard_map/all_gather | solution.py:55
  12.6 89.8 %all-gather.5.cloned.1.call-start = ((), (), s32[]{:S(2)}) async-start(), calls=%async_computation.1 | async-start | bytes 2228224 | tf_op jit(solution)/shard_map/all_gather | solution.py:54
  13.7 408.0 %all-reduce.3.cloned.1.call-start = ((), (), s32[]{:S(2)}) async-start(), calls=%async_computation.2 | async-start | bytes 8388608 | tf_op jit(solution)/shard_map/psum | solution.py:9
  64.6 0.7 copy-start.6
  421.6 4.3 copy-start.3
  421.6 4.3 copy-start.4
  425.1 1.1 copy-start.2
  425.1 1.1 copy-start.5
Sparse Core Ops, SparseCore 0:
  12.7 45.6 all-gather.2
  60.5 41.7 all-gather.4
  105.3 316.2 all-reduce.2
where the time goes:
time: 434 us
  waiting for transfers between devices  397 us (91%)
  between operations  13.3 us (3%)
  local copies, waits for them, and re-layouts  11.1 us (3%)
  other arithmetic  6.45 us (1%)
  matrix products  5.75 us (1%)
    psum x1, waiting for transfers between devices, from_root(): return lax.psum(jnp.where(mine, value, jnp.zeros_like(value)), axis)  315 us
    all_gather x1, waiting for transfers between devices, per_device(): lax.all_gather(right_tile, 'col', axis=1, tiled=True)  44.7 us
    all_gather x1, waiting for transfers between devices, per_device(): lax.all_gather(left_tile, 'col', axis=1, tiled=True)  36.9 us
  transfers between devices with their start and end apart: 3, of which 3 were waited for; matrix products, arithmetic and copies ran while one was open for 3% of the time, Pallas kernels for 0%

commit v1 on v0

v1 whole, which is shorter than its diff:
```python
import jax
import jax.numpy as jnp
from jax import lax
from jax.experimental import pallas as pl
from jax.experimental.pallas import tpu as pltpu
from jax.sharding import PartitionSpec as P

MESH = pl.DeviceIdType.MESH
F32 = jnp.float32
BF16 = jnp.bfloat16


def dot_nn(a, b):
    return lax.dot_general(a, b, (((1,), (0,)), ((), ())), preferred_element_type=F32)


def dot_nt(a, b):
    return lax.dot_general(a, b, (((1,), (1,)), ((), ())), preferred_element_type=F32)


def iota(shape, dim):
    return lax.broadcasted_iota(jnp.int32, shape, dim)


def eye(n):
    return (iota((n, n), 0) == iota((n, n), 1)).astype(F32).astype(BF16)


def layer_norm_lanes(values, gain, bias):
    mean = jnp.mean(values, axis=-1, keepdims=True)
    centred = values - mean
    var = jnp.mean(centred * centred, axis=-1, keepdims=True)
    return centred * lax.rsqrt(var + 1e-05) * gain + bias


def sigmoid(x):
    return 1.0 / (1.0 + jnp.exp(-x))


def project(pair, gain, bias, proj_w, proj_b):
    normed = layer_norm_lanes(pair.astype(F32), gain, bias).astype(BF16)
    proj = dot_nn(normed, proj_w) + proj_b
    left = (sigmoid(proj[:, :128]) * proj[:, 128:256]).astype(BF16)
    right = (sigmoid(proj[:, 256:384]) * proj[:, 384:]).astype(BF16)
    return normed, left, right


def interleave(parts, roll):
    parts = [p.reshape(16, 8, p.shape[-1]) for p in parts]
    turned = [roll(p, 4, 1) for p in parts]
    low = iota(parts[0].shape, 1) < 4
    even = [jnp.where(low, parts[a], turned[a + 1]) for a in (0, 2)]
    odd = [jnp.where(low, turned[a], parts[a + 1]) for a in (0, 2)]
    return jnp.concatenate(even, axis=1), jnp.concatenate(odd, axis=1)


def edges_out(edge, roll):
    turned = dot_nt(eye(128), edge)
    even, odd = interleave([turned[:, q * 128 : (q + 1) * 128] for q in range(4)], roll)
    return even.astype(BF16), odd.astype(BF16)


def relay(rows):
    return dot_nt(eye(128), rows).astype(BF16).reshape(4, 32, rows.shape[0])


def place_const():
    a, b = iota((512, 256), 0), iota((512, 256), 1)
    j4, c, zhi, rest = a // 128, (a // 64) % 2, (a // 32) % 2, a % 32
    goal = zhi * 128 + j4 * 32 + rest
    return [jnp.where((goal == b) & (c == core), 1.0, 0.0).astype(BF16) for core in range(2)]


def gather_const():
    a, b = iota((1024, 256), 0), iota((1024, 256), 1)
    i4, core, j4, zlo, q = a // 256, (a // 128) % 2, (a // 32) % 4, (a // 16) % 2, (a // 4) % 4
    goal = core * 128 + i4 * 32 + zlo * 16 + q * 4 + j4
    return jnp.where(goal == b, 1.0, 0.0).astype(BF16)


def right_operand(r_all, place):
    cat = jnp.concatenate([r_all[:, j].reshape(256, 128) for j in range(4)], axis=1)
    return jnp.concatenate([dot_nn(cat, place[c]).astype(BF16) for c in range(2)], axis=0)


def join(left, right, gather):
    keep = iota((256, 256), 0) % 4 == iota((256, 256), 1) % 4
    parts = []
    for block in left:
        both = lax.dot_general(block, right, (((0,), (0,)), ((), ())), preferred_element_type=F32)
        parts.append(jnp.where(keep, both, 0.0).astype(BF16))
    return dot_nn(jnp.concatenate(parts, axis=1), gather).astype(BF16)


def group_sum(x, roll):
    row = iota(x.shape, 0)
    x = x + jnp.where(row % 2 == 0, roll(x, 15, 0), roll(x, 1, 0))
    return x + jnp.where(row % 4 < 2, roll(x, 14, 0), roll(x, 2, 0))


def spread(value, roll):
    even, odd = interleave([value] * 4, roll)
    return jnp.stack([even, odd], axis=1).reshape(512, value.shape[-1])


def wide_weight(out_w, roll):
    rows = spread(out_w.astype(F32), roll)
    q = (iota(rows.shape, 0) // 4) % 4
    return jnp.concatenate([jnp.where(q == p, rows, 0.0) for p in range(4)], axis=1).astype(BF16)


def finish(joined, gain, bias, wide, out_b, roll):
    vals = joined.astype(F32).reshape(32, 16, 128)
    mean = group_sum(jnp.sum(vals, axis=0), roll) * (1.0 / 128)
    centred = vals - mean[None]
    var = group_sum(jnp.sum(centred * centred, axis=0), roll) * (1.0 / 128)
    scale = lax.rsqrt(var + 1e-05)
    normed = (centred * scale[None]).reshape(512, 128) * gain + bias
    turned = dot_nt(eye(128), normed.astype(BF16)).astype(BF16)
    value = dot_nn(turned, wide)
    return [value[:, q * 128 : (q + 1) * 128] + out_b for q in range(4)]


def kernel(
    pair_ref, in_gain, in_bias, proj_w, proj_b, norm_gain, norm_bias, out_w, out_b, gate_w, gate_b,
    out_ref,
    x_tx, x_rx, l_all, r_tx, r_all, t_tx, f_rx, gate_s, place_s, gather_s, wide_s, gain_s, bias_s,
    x_send, x_recv, l_send, l_recv, r_send, r_recv, f_send, f_recv,
):
    roll = pltpu.roll
    row, col = lax.axis_index("row"), lax.axis_index("col")
    y_hi, z = row // 16, row % 16
    y_lo, x, core = col // 8, (col // 2) % 4, col % 2
    chip = y_lo * 4 + x
    me = z * 2 + core

    barrier = pltpu.get_barrier_semaphore()

    def greet(device):
        pl.semaphore_signal(barrier, inc=1, device_id=device, device_id_type=MESH)

    def column(t):
        d = (me + t) % 32
        return d, (y_hi * 16 + d // 2, chip * 2 + d % 2)

    @pl.loop(1, 32)
    def _(t):
        greet(column(t)[1])

    here = y_hi * 8 + chip

    @pl.loop(1, 16)
    def _(t):
        p = (here + t) % 16
        greet(((p // 8) * 16 + z, (p % 8) * 2 + core))

    normed, left, right = project(
        pair_ref[...].reshape(512, 128), in_gain[...], in_bias[...], proj_w[...], proj_b[...]
    )
    for side, edge in enumerate((left, right)):
        even, odd = edges_out(edge, roll)
        even, odd = even.reshape(16, 1, 16, 128), odd.reshape(16, 1, 16, 128)
        x_tx[:, side] = jnp.concatenate([even, odd], axis=1)

    pl.semaphore_wait(barrier, 46)

    def edge_copy(d, device):
        return pltpu.make_async_remote_copy(
            src_ref=x_tx.at[d // 2, :, d % 2], dst_ref=x_rx.at[:, me], send_sem=x_send, recv_sem=x_recv,
            device_id=device, device_id_type=MESH,
        )

    @pl.loop(1, 32)
    def _(t):
        d, device = column(t)
        edge_copy(d, device).start()

    own = pltpu.make_async_copy(x_tx.at[z, :, core], x_rx.at[:, me], x_recv)
    own.start()

    gate_s[...] = sigmoid(dot_nn(normed, gate_w[...]) + gate_b[...])
    place = place_const()
    place_s[0], place_s[1] = place[0], place[1]
    gather_s[...] = gather_const()
    wide_s[...] = wide_weight(out_w[...], roll)
    gain_s[...] = spread(jnp.transpose(jnp.broadcast_to(norm_gain[...], (128, 128))), roll)
    bias_s[...] = spread(jnp.transpose(jnp.broadcast_to(norm_bias[...], (128, 128))), roll)

    pltpu.make_async_copy(x_rx, x_rx, x_recv).wait()

    got = x_rx[...].reshape(2, 16, 2, 16, 128)
    for c in range(2):
        l_all[:, c, chip] = relay(got[0, :, c].reshape(256, 128))

    def left_copy(t):
        p = (chip + t) % 8
        return pltpu.make_async_remote_copy(
            src_ref=l_all.at[:, :, chip], dst_ref=l_all.at[:, :, chip], send_sem=l_send, recv_sem=l_recv,
            device_id=(row, p * 2 + core), device_id_type=MESH,
        )

    @pl.loop(1, 8)
    def _(t):
        left_copy(t).start()

    for s in range(4):
        rows = jnp.concatenate(
            [got[1, 4 * s : 4 * s + 4, c].reshape(64, 128) for c in range(2)], axis=0
        )
        r_tx[s] = relay(rows)

    def right_copy(s, hi):
        return pltpu.make_async_remote_copy(
            src_ref=r_tx.at[s], dst_ref=r_all.at[chip], send_sem=r_send, recv_sem=r_recv,
            device_id=(hi * 16 + z, y_hi * 8 + s * 2 + core), device_id_type=MESH,
        )

    def is_own(s, hi):
        return (hi == y_hi) & (y_lo == y_hi) & (s == x)

    @pl.loop(0, 8)
    def _(t):
        s, hi = t % 4, t // 4
        same = is_own(s, hi)

        @pl.when(same)
        def _():
            pltpu.make_async_copy(r_tx.at[s], r_all.at[chip], r_recv).start()

        @pl.when(jnp.logical_not(same))
        def _():
            right_copy(s, hi).start()

    pltpu.make_async_copy(r_all, r_all, r_recv).wait()
    operand = right_operand(r_all[...], [place_s[0], place_s[1]])
    seven = l_all.at[:, :, pl.ds(0, 7)]
    pltpu.make_async_copy(seven, seven, l_recv).wait()

    joined = join([l_all[i].reshape(512, 256) for i in range(4)], operand, gather_s[...])
    for c in range(2):
        t_tx[:, c] = joined[:, c * 128 : (c + 1) * 128].reshape(16, 16, 128)

    def back_copy(d, device):
        return pltpu.make_async_remote_copy(
            src_ref=t_tx.at[d // 2, d % 2], dst_ref=f_rx.at[me], send_sem=f_send, recv_sem=f_recv,
            device_id=device, device_id_type=MESH,
        )

    @pl.loop(1, 32)
    def _(t):
        d, device = column(t)
        back_copy(d, device).start()

    pltpu.make_async_copy(t_tx.at[z, core], f_rx.at[me], f_recv).start()
    pltpu.make_async_copy(f_rx, f_rx, f_recv).wait()

    values = finish(f_rx[...].reshape(512, 128), gain_s[...], bias_s[...], wide_s[...], out_b[...], roll)
    for q in range(4):
        update = values[q] * gate_s[q * 128 : (q + 1) * 128]
        out_ref[4 * q : 4 * q + 4] = update.astype(BF16).reshape(4, 32, 128)

    @pl.loop(1, 32)
    def _(t):
        d, device = column(t)
        edge_copy(d, device).wait_send()
        back_copy(d, device).wait_send()

    @pl.loop(1, 8)
    def _(t):
        left_copy(t).wait_send()

    @pl.loop(0, 8)
    def _(t):
        s, hi = t % 4, t // 4

        @pl.when(jnp.logical_not(is_own(s, hi)))
        def _():
            right_copy(s, hi).wait_send()


def per_device(pair, in_gain, in_bias, proj_w, proj_b, norm_gain, norm_bias, out_w, out_b, gate_w, gate_b):
    def flat(v):
        return v.reshape(1, -1)

    vmem = pl.BlockSpec(memory_space=pltpu.VMEM)
    dma = pltpu.SemaphoreType.DMA
    return pl.pallas_call(
        kernel,
        out_shape=jax.ShapeDtypeStruct(pair.shape, BF16),
        in_specs=[vmem] * 11,
        out_specs=vmem,
        scratch_shapes=[
            pltpu.VMEM((16, 2, 2, 16, 128), BF16),
            pltpu.VMEM((2, 32, 16, 128), BF16),
            pltpu.VMEM((4, 2, 8, 32, 256), BF16),
            pltpu.VMEM((4, 4, 32, 128), BF16),
            pltpu.VMEM((8, 4, 32, 128), BF16),
            pltpu.VMEM((16, 2, 16, 128), BF16),
            pltpu.VMEM((32, 16, 128), BF16),
            pltpu.VMEM((512, 128), F32),
            pltpu.VMEM((2, 512, 256), BF16),
            pltpu.VMEM((1024, 256), BF16),
            pltpu.VMEM((512, 512), BF16),
            pltpu.VMEM((512, 128), F32),
            pltpu.VMEM((512, 128), F32),
        ]
        + [dma] * 8,
        compiler_params=pltpu.CompilerParams(
            collective_id=0, has_side_effects=True, vmem_limit_bytes=40 * 1024 * 1024
        ),
    )(
        pair, flat(in_gain), flat(in_bias), proj_w, flat(proj_b), flat(norm_gain), flat(norm_bias),
        out_w, flat(out_b), gate_w, flat(gate_b),
    )


def solution(mesh):
    return jax.shard_map(
        per_device,
        mesh=mesh,
        in_specs=(P("row", "col", None), P(), P(), P(), P(), P(), P(), P(), P(), P(), P()),
        out_specs=P("row", "col", None),
        check_vma=False,
    )
```

time: 434 us -> 69.8 us (0.16)
  the two profiles are of different devices: /device:TPU:2 before, /device:TPU:1 now
where the time goes in v1:
time: 69.8 us; the launch traced here: 68.6 us
  Pallas kernels  63.9 us (92%)
  local copies, waits for them, and re-layouts  4.69 us (7%)
    pallas_call x1, Pallas kernels, per_device(): pl.pallas_call(kernel, out_shape=jax.ShapeDtypeStruct(pair.shape, BF16),...  63.9 us
    unnamed x23, local copies, waits for them, and re-layouts  4.69 us

profile of v1, /device:TPU:1, one launch (start us, length us, event | category | flops | bytes accessed | tf_op | source)
XLA Modules:
  0.0 68.6 jit_solution(7889914229563967907)
XLA Ops:
  0.0 0.0 copy-start.8
  0.0 0.0 copy-start.9
  0.0 0.0 copy-start.10
  0.0 0.0 copy-start.4
  0.0 0.0 copy-start.5
  0.0 0.0 copy-start.6
  0.0 0.0 copy-start.7
  0.0 0.6 copy-done.8
  0.7 0.0 copy-done.9
  0.7 0.0 copy-done.10
  0.7 0.0 copy-done.4
  0.7 0.0 copy-done.5
  0.7 0.0 copy-done.6
  0.7 0.0 copy-done.7
  0.8 0.0 copy-start
  0.8 0.9 %copy-done = bf16[16,32,128]{2,1,0:T(8,128)(2,1)S(1)} copy-done((bf16[16,32,128]{2,1,0:T(8,128)(2,1)S(1)}, bf16[16,32,128]{2,1,0:T(8,128)(2,1)}, u32[]{:S(2)}) %copy-start) | copy-done | bytes 131096
  1.7 0.0 copy-start.1
  1.7 0.9 %copy-done.1 = bf16[128,512]{1,0:T(8,128)(2,1)S(1)} copy-done((bf16[128,512]{1,0:T(8,128)(2,1)S(1)}, bf16[128,512]{1,0:T(8,128)(2,1)}, u32[]{:S(2)}) %copy-start.1) | copy-done | bytes 131096
  2.6 0.0 copy-start.2
  2.6 0.8 %copy-done.2 = bf16[128,128]{1,0:T(8,128)(2,1)S(1)} copy-done((bf16[128,128]{1,0:T(8,128)(2,1)S(1)}, bf16[128,128]{1,0:T(8,128)(2,1)}, u32[]{:S(2)}) %copy-start.2) | copy-done | bytes 32792
  3.3 0.0 copy-start.3
  3.3 0.8 %copy-done.3 = bf16[128,128]{1,0:T(8,128)(2,1)S(1)} copy-done((bf16[128,128]{1,0:T(8,128)(2,1)S(1)}, bf16[128,128]{1,0:T(8,128)(2,1)}, u32[]{:S(2)}) %copy-start.3) | copy-done | bytes 32792
  4.1 63.9 %shard_map.109 = bf16[16,32,128]{2,1,0:T(8,128)(2,1)S(1)} custom-call(bf16[16,32,128]{2,1,0:T(8,128)(2,1)S(1)} %copy-done, f32[1,128]{1,0:T(1,128)S(1)} %bitcast.8, f32[1,128]{1,0:T(1,128)S(1)} %bitcast.9, bf16[128,512]{1,0:T(8,128)(2,1)S(1)} %copy-done.1, f32[1,512]{1,0:T(1,128)S(1)} %bitcast.7, f32[1,128]{1,0:T(1,128)S(1)} %bitcast.10, ...), custom_call_target="tpu_custom_call" | custom-call | tf_op jit(solution)/shard_map/pallas_call | solution.py:287
  67.9 0.7 copy.13
Async XLA Ops:
  0.0 0.7 copy-start.8
  0.0 0.7 copy-start.9
  0.0 0.7 copy-start.10
  0.0 0.7 %copy-start.4 = (f32[512]{0:T(512)S(1)}, f32[512]{0:T(512)}, u32[]{:S(2)}) copy-start(f32[512]{0:T(512)} %param.15) | copy-start | bytes 6148
  0.0 0.7 %copy-start.5 = (f32[128]{0:T(128)S(1)}, f32[128]{0:T(128)}, u32[]{:S(2)}) copy-start(f32[128]{0:T(128)} %param.12) | copy-start | bytes 1540
  0.0 0.7 %copy-start.6 = (f32[128]{0:T(128)S(1)}, f32[128]{0:T(128)}, u32[]{:S(2)}) copy-start(f32[128]{0:T(128)} %param.13) | copy-start | bytes 1540
  0.0 0.7 %copy-start.7 = (f32[128]{0:T(128)S(1)}, f32[128]{0:T(128)}, u32[]{:S(2)}) copy-start(f32[128]{0:T(128)} %param.16) | copy-start | bytes 1540
  0.8 0.9 %copy-start = (bf16[16,32,128]{2,1,0:T(8,128)(2,1)S(1)}, bf16[16,32,128]{2,1,0:T(8,128)(2,1)}, u32[]{:S(2)}) copy-start(bf16[16,32,128]{2,1,0:T(8,128)(2,1)} %pair_ref.1) | copy-start | bytes 393220
  1.7 0.9 %copy-start.1 = (bf16[128,512]{1,0:T(8,128)(2,1)S(1)}, bf16[128,512]{1,0:T(8,128)(2,1)}, u32[]{:S(2)}) copy-start(bf16[128,512]{1,0:T(8,128)(2,1)} %proj_w.1) | copy-start | bytes 393220
  2.6 0.8 %copy-start.2 = (bf16[128,128]{1,0:T(8,128)(2,1)S(1)}, bf16[128,128]{1,0:T(8,128)(2,1)}, u32[]{:S(2)}) copy-start(bf16[128,128]{1,0:T(8,128)(2,1)} %out_w.1) | copy-start | bytes 98308
  3.3 0.8 %copy-start.3 = (bf16[128,128]{1,0:T(8,128)(2,1)S(1)}, bf16[128,128]{1,0:T(8,128)(2,1)}, u32[]{:S(2)}) copy-start(bf16[128,128]{1,0:T(8,128)(2,1)} %gate_w.1) | copy-start | bytes 98308

commit v2 on v1

v2 whole, which is shorter than its diff:
```python
import jax
import jax.numpy as jnp
from jax import lax
from jax.experimental import pallas as pl
from jax.experimental.pallas import tpu as pltpu
from jax.sharding import PartitionSpec as P

MESH = pl.DeviceIdType.MESH
F32 = jnp.float32
BF16 = jnp.bfloat16


def dot_nn(a, b):
    return lax.dot_general(a, b, (((1,), (0,)), ((), ())), preferred_element_type=F32)


def dot_nt(a, b):
    return lax.dot_general(a, b, (((1,), (1,)), ((), ())), preferred_element_type=F32)


def iota(shape, dim):
    return lax.broadcasted_iota(jnp.int32, shape, dim)


def eye(n):
    return (iota((n, n), 0) == iota((n, n), 1)).astype(F32).astype(BF16)


def layer_norm_lanes(values, gain, bias):
    mean = jnp.mean(values, axis=-1, keepdims=True)
    centred = values - mean
    var = jnp.mean(centred * centred, axis=-1, keepdims=True)
    return centred * lax.rsqrt(var + 1e-05) * gain + bias


def sigmoid(x):
    return 1.0 / (1.0 + jnp.exp(-x))


def project(pair, gain, bias, proj_w, proj_b):
    normed = layer_norm_lanes(pair.astype(F32), gain, bias).astype(BF16)
    proj = dot_nn(normed, proj_w) + proj_b
    left = (sigmoid(proj[:, :128]) * proj[:, 128:256]).astype(BF16)
    right = (sigmoid(proj[:, 256:384]) * proj[:, 384:]).astype(BF16)
    return normed, left, right


def interleave(parts, roll):
    parts = [p.reshape(16, 8, p.shape[-1]) for p in parts]
    turned = [roll(p, 4, 1) for p in parts]
    low = iota(parts[0].shape, 1) < 4
    even = [jnp.where(low, parts[a], turned[a + 1]) for a in (0, 2)]
    odd = [jnp.where(low, turned[a], parts[a + 1]) for a in (0, 2)]
    return jnp.concatenate(even, axis=1), jnp.concatenate(odd, axis=1)


def edges_out(edge, roll):
    turned = dot_nt(eye(128), edge)
    even, odd = interleave([turned[:, q * 128 : (q + 1) * 128] for q in range(4)], roll)
    return even.astype(BF16), odd.astype(BF16)


def relay_left(rows):
    return dot_nt(eye(128), rows).astype(BF16).reshape(4, 32, 128)


def relay_right(rows):
    twice = jnp.concatenate([rows, rows], axis=0)
    r, c = iota((64, 128), 0), iota((64, 128), 1)
    base = (r // 32) * 64 + r % 32
    halves = [dot_nt(jnp.where(c == base + 32 * p, 1.0, 0.0).astype(BF16), twice) for p in range(2)]
    return jnp.where(c < 64, halves[0], halves[1]).astype(BF16).reshape(2, 32, 128)


def gather_const():
    a, b = iota((1024, 256), 0), iota((1024, 256), 1)
    i4, j4, core, zlo, q = a // 256, (a // 64) % 4, (a // 32) % 2, (a // 16) % 2, (a // 4) % 4
    goal = core * 128 + i4 * 32 + zlo * 16 + q * 4 + j4
    return jnp.where(goal == b, 1.0, 0.0).astype(BF16)


def join(left, right, offset, gather):
    keep = iota((128, 256), 0) % 4 == iota((128, 256), 1) % 4
    offset = jnp.concatenate([offset] * 8, axis=0)
    offset = jnp.concatenate([offset, offset], axis=1)
    parts = []
    for block in left:
        both = lax.dot_general(block, right, (((0,), (0,)), ((), ())), preferred_element_type=F32)
        parts.append(jnp.where(keep, both - offset, 0.0).astype(BF16))
    return dot_nn(jnp.concatenate(parts, axis=1), gather).astype(BF16)


def estimate(in_gain, in_bias, proj_w, proj_b):
    w = proj_w.astype(F32)

    def times(v, m):
        return dot_nn(jnp.concatenate([v] * 8, axis=0), m)[:1]

    mean = times(in_bias, w) + proj_b
    power = in_gain * in_gain
    total = 4.0 * 128.0
    for first in (0, 256):
        g, v = w[:, first : first + 128], w[:, first + 128 : first + 256]
        scale = lax.rsqrt(1.0 + (jnp.pi / 8) * times(power, g * g))
        gate = sigmoid(mean[:, first : first + 128] * scale)
        total = total * (
            gate * mean[:, first + 128 : first + 256] + times(power, g * v) * gate * (1.0 - gate) * scale
        )
    return total


def column(row):
    return jnp.transpose(jnp.broadcast_to(row, (128, 128)))


def group_sum(x, roll):
    row = iota(x.shape, 0)
    x = x + jnp.where(row % 2 == 0, roll(x, 15, 0), roll(x, 1, 0))
    return x + jnp.where(row % 4 < 2, roll(x, 14, 0), roll(x, 2, 0))


def spread(value, roll):
    even, odd = interleave([value] * 4, roll)
    return jnp.stack([even, odd], axis=1).reshape(512, value.shape[-1])


def wide_weight(out_w, roll):
    rows = spread(out_w.astype(F32), roll)
    q = (iota(rows.shape, 0) // 4) % 4
    return jnp.concatenate([jnp.where(q == p, rows, 0.0) for p in range(4)], axis=1).astype(BF16)


def finish(joined, offset, gain, bias, wide, out_b, roll):
    vals = (joined.astype(F32) + offset).reshape(32, 16, 128)
    mean = group_sum(jnp.sum(vals, axis=0), roll) * (1.0 / 128)
    centred = vals - mean[None]
    var = group_sum(jnp.sum(centred * centred, axis=0), roll) * (1.0 / 128)
    scale = lax.rsqrt(var + 1e-05)
    normed = (centred * scale[None]).reshape(512, 128) * gain + bias
    turned = dot_nt(eye(128), normed.astype(BF16)).astype(BF16)
    value = dot_nn(turned, wide)
    return [value[:, q * 128 : (q + 1) * 128] + out_b for q in range(4)]


N_IN = 11
NEAR = (4, 13, 3, 14, 2, 15, 1)
FAR = (8, 7, 9, 6, 10, 5, 11, 12)


def kernel(*refs):
    hbm, out_ref, held, rest = refs[:N_IN], refs[N_IN], refs[N_IN + 1 : 2 * N_IN + 1], refs[2 * N_IN + 1 :]
    pair, in_gain, in_bias, proj_w, proj_b, norm_gain, norm_bias, out_w, out_b, gate_w, gate_b = held
    (
        x_tx, x_rx, y_tx, l_all, r_tx, r_all, t_tx, u_all, f_rx, gate_s, gather_s, wide_s, gain_s, bias_s, off_s,
        in_sem, x_send, x_recv, l_send, l_recv, r_send, r_recv, t_send, t_recv, f_send, f_recv,
    ) = rest
    roll = pltpu.roll
    fetch = [pltpu.make_async_copy(hbm[n], held[n], in_sem.at[n]) for n in range(N_IN)]
    for copy in fetch:
        copy.start()

    row, col = lax.axis_index("row"), lax.axis_index("col")
    y_hi, z = lax.div(row, 16), lax.rem(row, 16)
    y_lo, x, core = lax.div(col, 8), lax.rem(lax.div(col, 2), 4), lax.rem(col, 2)
    barrier = pltpu.get_barrier_semaphore()

    def along_z(off):
        return lax.rem(z + off, 16)

    def greet(device):
        pl.semaphore_signal(barrier, inc=1, device_id=device, device_id_type=MESH)

    for off in FAR + NEAR:
        greet((y_hi * 16 + along_z(off), col))

    @pl.loop(1, 32)
    def _(t):
        p = lax.rem(y_hi * 16 + col + t, 32)
        greet((lax.div(p, 16) * 16 + z, lax.rem(p, 16)))

    for n in range(5):
        fetch[n].wait()
    normed, left, right = project(
        pair[...].reshape(512, 128), in_gain[...], in_bias[...], proj_w[...], proj_b[...]
    )
    for side, edge in enumerate((left, right)):
        even, odd = edges_out(edge, roll)
        x_tx[side] = jnp.concatenate([even.reshape(16, 1, 16, 128), odd.reshape(16, 1, 16, 128)], axis=1)

    pl.semaphore_wait(barrier, 46)

    def edge_copy(side, off):
        there = along_z(off)
        group = 2 if side else int((4 - off) % 16 >= 8)
        slot = z if side else (4 - off) % 16
        return pltpu.make_async_remote_copy(
            src_ref=x_tx.at[side, there], dst_ref=x_rx.at[side, slot], send_sem=x_send,
            recv_sem=x_recv.at[group], device_id=(y_hi * 16 + there, col), device_id_type=MESH,
        )

    pltpu.make_async_copy(x_tx.at[0, z], x_rx.at[0, 4], x_recv.at[0]).start()
    for off in NEAR + FAR:
        edge_copy(0, off).start()
    pltpu.make_async_copy(x_tx.at[1, z], x_rx.at[1, z], x_recv.at[2]).start()
    for off in FAR + NEAR:
        edge_copy(1, off).start()

    for n in range(5, N_IN):
        fetch[n].wait()
    gate_s[...] = sigmoid(dot_nn(normed, gate_w[...]) + gate_b[...])

    def left_copy(group, t):
        p = lax.rem(col + t, 16)
        return pltpu.make_async_remote_copy(
            src_ref=y_tx.at[group, lax.rem(p, 2)], dst_ref=l_all.at[group, col], send_sem=l_send,
            recv_sem=l_recv.at[group], device_id=(row, p), device_id_type=MESH,
        )

    for group in range(2):
        part = x_rx.at[0, pl.ds(8 * group, 8)]
        pltpu.make_async_copy(part, part, x_recv.at[group]).wait()
        for c in range(2):
            y_tx[group, c] = relay_left(x_rx[0, 8 * group : 8 * group + 8, c].reshape(128, 128))
        l_all[group, col] = y_tx[group, core]

        @pl.loop(1, 16)
        def _(t):
            left_copy(group, t).start()

    def right_copy(t):
        s, c, hi = lax.rem(t, 4), lax.rem(lax.div(t, 4), 2), lax.div(t, 8)
        there = (hi * 16 + z, y_hi * 8 + s * 2 + c)
        same = (there[0] == row) & (there[1] == col)
        return same, r_tx.at[s, c], pltpu.make_async_remote_copy(
            src_ref=r_tx.at[s, c], dst_ref=r_all.at[col], send_sem=r_send, recv_sem=r_recv,
            device_id=there, device_id_type=MESH,
        )

    part = x_rx.at[1]
    pltpu.make_async_copy(part, part, x_recv.at[2]).wait()
    for s in range(4):
        for c in range(2):
            r_tx[s, c] = relay_right(x_rx[1, 4 * s : 4 * s + 4, c].reshape(64, 128))

    @pl.loop(0, 16)
    def _(t):
        same, here, copy = right_copy(t)

        @pl.when(same)
        def _():
            pltpu.make_async_copy(here, r_all.at[col], r_recv).start()

        @pl.when(jnp.logical_not(same))
        def _():
            copy.start()

    gather_s[...] = gather_const()
    off_s[...] = spread(column(estimate(in_gain[...], in_bias[...], proj_w[...], proj_b[...])), roll)
    wide_s[...] = wide_weight(out_w[...], roll)
    gain_s[...] = spread(column(norm_gain[...]), roll)
    bias_s[...] = spread(column(norm_bias[...]), roll)
    offset = off_s[pl.ds(pl.multiple_of((z * 2 + core) * 16, 16), 16), :]

    pltpu.make_async_copy(r_all, r_all, r_recv).wait()
    operand = jnp.concatenate([r_all[:, 0].reshape(512, 128), r_all[:, 1].reshape(512, 128)], axis=1)

    def sibling_copy(group):
        return pltpu.make_async_remote_copy(
            src_ref=t_tx.at[group], dst_ref=u_all.at[pl.ds(8 * group, 8), core], send_sem=t_send,
            recv_sem=t_recv.at[group], device_id=(row, col + 1 - 2 * core), device_id_type=MESH,
        )

    def back_copy(off):
        there = along_z(off)
        return pltpu.make_async_remote_copy(
            src_ref=u_all.at[(off + 4) % 16], dst_ref=f_rx.at[z], send_sem=f_send, recv_sem=f_recv,
            device_id=(y_hi * 16 + there, col), device_id_type=MESH,
        )

    for group in range(2):
        part = l_all.at[group, pl.ds(0, 15)]
        pltpu.make_async_copy(part, part, l_recv.at[group]).wait()
        joined = join(
            [l_all[group, :, i].reshape(512, 128) for i in range(4)], operand, offset, gather_s[...]
        ).reshape(8, 16, 256)
        low, high = joined[:, :, :128], joined[:, :, 128:]
        first = core == 0
        t_tx[group] = jnp.where(first, high, low)
        sibling_copy(group).start()
        u_all[8 * group : 8 * group + 8, core] = jnp.where(first, low, high)
        part = u_all.at[pl.ds(8 * group, 8), 1 - core]
        pltpu.make_async_copy(part, part, t_recv.at[group]).wait()
        for off in FAR + NEAR:
            if (off + 4) % 16 // 8 == group:
                back_copy(off).start()
    pltpu.make_async_copy(u_all.at[4], f_rx.at[z], f_recv).start()

    pltpu.make_async_copy(f_rx, f_rx, f_recv).wait()
    values = finish(
        f_rx[...].reshape(512, 128), off_s[...], gain_s[...], bias_s[...], wide_s[...], out_b[...], roll
    )
    for q in range(4):
        update = values[q] * gate_s[q * 128 : (q + 1) * 128]
        out_ref[4 * q : 4 * q + 4] = update.astype(BF16).reshape(4, 32, 128)

    for off in NEAR + FAR:
        edge_copy(0, off).wait_send()
        edge_copy(1, off).wait_send()
        back_copy(off).wait_send()
    for group in range(2):
        sibling_copy(group).wait_send()

        @pl.loop(1, 16)
        def _(t):
            left_copy(group, t).wait_send()

    @pl.loop(0, 16)
    def _(t):
        same, _, copy = right_copy(t)

        @pl.when(jnp.logical_not(same))
        def _():
            copy.wait_send()


def per_device(*args):
    args = [a.reshape(1, -1) if a.ndim == 1 else a for a in args]
    dma = pltpu.SemaphoreType.DMA
    return pl.pallas_call(
        kernel,
        out_shape=jax.ShapeDtypeStruct(args[0].shape, BF16),
        in_specs=[pl.BlockSpec(memory_space=pl.ANY)] * N_IN,
        out_specs=pl.BlockSpec(memory_space=pltpu.VMEM),
        scratch_shapes=[pltpu.VMEM(a.shape, a.dtype) for a in args]
        + [
            pltpu.VMEM((2, 16, 2, 16, 128), BF16),
            pltpu.VMEM((2, 16, 2, 16, 128), BF16),
            pltpu.VMEM((2, 2, 4, 32, 128), BF16),
            pltpu.VMEM((2, 16, 4, 32, 128), BF16),
            pltpu.VMEM((4, 2, 2, 32, 128), BF16),
            pltpu.VMEM((16, 2, 32, 128), BF16),
            pltpu.VMEM((2, 8, 16, 128), BF16),
            pltpu.VMEM((16, 2, 16, 128), BF16),
            pltpu.VMEM((16, 2, 16, 128), BF16),
            pltpu.VMEM((512, 128), F32),
            pltpu.VMEM((1024, 256), BF16),
            pltpu.VMEM((512, 512), BF16),
            pltpu.VMEM((512, 128), F32),
            pltpu.VMEM((512, 128), F32),
            pltpu.VMEM((512, 128), F32),
            dma((N_IN,)), dma, dma((3,)), dma, dma((2,)), dma, dma, dma, dma((2,)), dma, dma,
        ],
        compiler_params=pltpu.CompilerParams(
            collective_id=0, has_side_effects=True, vmem_limit_bytes=56 * 1024 * 1024
        ),
    )(*args)


def solution(mesh):
    return jax.shard_map(
        per_device,
        mesh=mesh,
        in_specs=(P("row", "col", None), P(), P(), P(), P(), P(), P(), P(), P(), P(), P()),
        out_specs=P("row", "col", None),
        check_vma=False,
    )
```

time: 69.8 us -> 52.5 us (0.75)
  Pallas kernels: 63.9 us -> 50.2 us
  local copies, waits for them, and re-layouts: 4.69 us -> 1.57 us
    pallas_call x1, Pallas kernels: 63.9 us -> 50.2 us  [per_device(): pl.pallas_call(kernel, out_shape=jax.ShapeDtypeStruct(args[0].shape, BF16...]
    unnamed x23 -> x1, local copies, waits for them, and re-layouts: 4.69 us -> 1.57 us
where the time goes in v2:
time: 52.5 us; the launch traced here: 51.8 us
  Pallas kernels  50.2 us (96%)
  local copies, waits for them, and re-layouts  1.57 us (3%)
    pallas_call x1, Pallas kernels, per_device(): pl.pallas_call(kernel, out_shape=jax.ShapeDtypeStruct(args[0].shape, BF16...  50.2 us
    unnamed x1, local copies, waits for them, and re-layouts  1.57 us

profile of v2, /device:TPU:1, one launch (start us, length us, event | category | flops | bytes accessed | tf_op | source)
XLA Modules:
  0.0 51.8 jit_solution(3262879102402357908)
XLA Ops:
  0.0 50.2 %shard_map.109 = bf16[16,32,128]{2,1,0:T(8,128)(2,1)} custom-call(bf16[16,32,128]{2,1,0:T(8,128)(2,1)} %refs_0_.1, f32[1,128]{1,0:T(1,128)} %bitcast.8, f32[1,128]{1,0:T(1,128)} %bitcast.9, bf16[128,512]{1,0:T(8,128)(2,1)} %refs_3_.1, f32[1,512]{1,0:T(1,128)} %bitcast.7, f32[1,128]{1,0:T(1,128)} %bitcast.10, f32[1,128]{1,0:T(1,128)} %bitcast.11, ...), custom_call_target="tpu_custom_call" | custom-call | tf_op jit(solution)/shard_map/pallas_call | solution.py:329
  50.2 1.6 %copy.13 = bf16[16,32,128]{2,1,0:T(8,128)(2,1)} copy(bf16[16,32,128]{2,1,0:T(8,128)(2,1)} %shard_map.109) | data formatting | bytes 262144

commit v3 on v2

v3 whole, which is shorter than its diff:
```python
import jax
import jax.numpy as jnp
from jax import lax
from jax.experimental import pallas as pl
from jax.experimental.pallas import tpu as pltpu
from jax.sharding import PartitionSpec as P

MESH = pl.DeviceIdType.MESH
F32 = jnp.float32
BF16 = jnp.bfloat16


def dot_nn(a, b):
    return lax.dot_general(a, b, (((1,), (0,)), ((), ())), preferred_element_type=F32)


def dot_nt(a, b):
    return lax.dot_general(a, b, (((1,), (1,)), ((), ())), preferred_element_type=F32)


def iota(shape, dim):
    return lax.broadcasted_iota(jnp.int32, shape, dim)


def eye(n):
    return (iota((n, n), 0) == iota((n, n), 1)).astype(F32).astype(BF16)


def layer_norm_lanes(values, gain, bias):
    mean = jnp.mean(values, axis=-1, keepdims=True)
    centred = values - mean
    var = jnp.mean(centred * centred, axis=-1, keepdims=True)
    return centred * lax.rsqrt(var + 1e-05) * gain + bias


def sigmoid(x):
    return 1.0 / (1.0 + jnp.exp(-x))


def project(pair, gain, bias, proj_w, proj_b):
    normed = layer_norm_lanes(pair.astype(F32), gain, bias).astype(BF16)
    proj = dot_nn(normed, proj_w) + proj_b
    left = (sigmoid(proj[:, :128]) * proj[:, 128:256]).astype(BF16)
    right = (sigmoid(proj[:, 256:384]) * proj[:, 384:]).astype(BF16)
    return normed, left, right


def interleave(parts, roll):
    parts = [p.reshape(16, 8, p.shape[-1]) for p in parts]
    turned = [roll(p, 4, 1) for p in parts]
    low = iota(parts[0].shape, 1) < 4
    even = [jnp.where(low, parts[a], turned[a + 1]) for a in (0, 2)]
    odd = [jnp.where(low, turned[a], parts[a + 1]) for a in (0, 2)]
    return jnp.concatenate(even, axis=1), jnp.concatenate(odd, axis=1)


def edges_out(edge, roll):
    turned = dot_nt(eye(128), edge)
    even, odd = interleave([turned[:, q * 128 : (q + 1) * 128] for q in range(4)], roll)
    return even.astype(BF16), odd.astype(BF16)


def relay_left(rows):
    return dot_nt(eye(128), rows).astype(BF16).reshape(4, 32, 128)


def relay_right(rows):
    twice = jnp.concatenate([rows, rows], axis=0)
    r, c = iota((64, 128), 0), iota((64, 128), 1)
    base = (r // 32) * 64 + r % 32
    halves = [dot_nt(jnp.where(c == base + 32 * p, 1.0, 0.0).astype(BF16), twice) for p in range(2)]
    return jnp.where(c < 64, halves[0], halves[1]).astype(BF16).reshape(2, 32, 128)


def gather_const():
    a, b = iota((1024, 256), 0), iota((1024, 256), 1)
    i4, j4, core, zlo, q = a // 256, (a // 64) % 4, (a // 32) % 2, (a // 16) % 2, (a // 4) % 4
    goal = core * 128 + i4 * 32 + zlo * 16 + q * 4 + j4
    return jnp.where(goal == b, 1.0, 0.0).astype(BF16)


def join(left, right, gather):
    keep = iota((128, 256), 0) % 4 == iota((128, 256), 1) % 4
    high, low = [], []
    for block in left:
        both = lax.dot_general(block, right, (((0,), (0,)), ((), ())), preferred_element_type=F32)
        both = jnp.where(keep, both, 0.0)
        high.append(both.astype(BF16))
        low.append((both - high[-1].astype(F32)).astype(BF16))
    return dot_nn(jnp.concatenate(high, axis=1), gather) + dot_nn(jnp.concatenate(low, axis=1), gather)


def estimate(in_gain, in_bias, proj_w, proj_b):
    w = proj_w.astype(F32)

    def times(v, m):
        return dot_nn(jnp.concatenate([v] * 8, axis=0), m)[:1]

    mean = times(in_bias, w) + proj_b
    power = in_gain * in_gain
    total = 4.0 * 128.0
    for first in (0, 256):
        g, v = w[:, first : first + 128], w[:, first + 128 : first + 256]
        scale = lax.rsqrt(1.0 + (jnp.pi / 8) * times(power, g * g))
        gate = sigmoid(mean[:, first : first + 128] * scale)
        total = total * (
            gate * mean[:, first + 128 : first + 256] + times(power, g * v) * gate * (1.0 - gate) * scale
        )
    return total


def column(row):
    return jnp.transpose(jnp.broadcast_to(row, (128, 128)))


def group_sum(x, roll):
    row = iota(x.shape, 0)
    x = x + jnp.where(row % 2 == 0, roll(x, 15, 0), roll(x, 1, 0))
    return x + jnp.where(row % 4 < 2, roll(x, 14, 0), roll(x, 2, 0))


def spread(value, roll):
    even, odd = interleave([value] * 4, roll)
    return jnp.stack([even, odd], axis=1).reshape(512, value.shape[-1])


def wide_weight(out_w, roll):
    rows = spread(out_w.astype(F32), roll)
    q = (iota(rows.shape, 0) // 4) % 4
    return jnp.concatenate([jnp.where(q == p, rows, 0.0) for p in range(4)], axis=1).astype(BF16)


def finish(joined, offset, gain, bias, wide, out_b, roll):
    vals = (joined.astype(F32) + offset).reshape(32, 16, 128)
    mean = group_sum(jnp.sum(vals, axis=0), roll) * (1.0 / 128)
    centred = vals - mean[None]
    var = group_sum(jnp.sum(centred * centred, axis=0), roll) * (1.0 / 128)
    scale = lax.rsqrt(var + 1e-05)
    normed = (centred * scale[None]).reshape(512, 128) * gain + bias
    turned = dot_nt(eye(128), normed.astype(BF16)).astype(BF16)
    value = dot_nn(turned, wide)
    return [value[:, q * 128 : (q + 1) * 128] + out_b for q in range(4)]


N_IN = 11
ORDER = (8, 7, 9, 6, 10, 5, 11, 4, 12, 3, 13, 2, 14, 1, 15)


def kernel(*refs):
    hbm, out_ref, held, rest = refs[:N_IN], refs[N_IN], refs[N_IN + 1 : 2 * N_IN + 1], refs[2 * N_IN + 1 :]
    pair, in_gain, in_bias, proj_w, proj_b, norm_gain, norm_bias, out_w, out_b, gate_w, gate_b = held
    (
        x_tx, x_rx, l_all, r_tx, r_all, t_own, t_tx, t_rx, u_all, f_rx, gate_s, gather_s, wide_s, gain_s, bias_s, off_s,
        in_sem, x_send, x_recv, l_send, l_recv, r_send, r_recv, t_send, t_recv, f_send, f_recv,
    ) = rest
    roll = pltpu.roll
    fetch = [pltpu.make_async_copy(hbm[n], held[n], in_sem.at[n]) for n in range(N_IN)]
    for copy in fetch:
        copy.start()

    row, col = lax.axis_index("row"), lax.axis_index("col")
    y_hi, z = lax.div(row, 16), lax.rem(row, 16)
    y_lo, x, core = lax.div(col, 8), lax.rem(lax.div(col, 2), 4), lax.rem(col, 2)
    chip = y_lo * 4 + x
    barrier = pltpu.get_barrier_semaphore()

    def along_z(off):
        return lax.rem(z + off, 16)

    def greet(device):
        pl.semaphore_signal(barrier, inc=1, device_id=device, device_id_type=MESH)

    for off in ORDER:
        greet((y_hi * 16 + along_z(off), col))
    for t in range(1, 16):
        p = lax.rem(y_hi * 8 + chip + t, 16)
        greet((lax.div(p, 8) * 16 + z, lax.rem(p, 8) * 2 + core))
    sibling = (row, col + 1 - 2 * core)
    greet(sibling)

    for n in range(5):
        fetch[n].wait()
    normed, left, right = project(
        pair[...].reshape(512, 128), in_gain[...], in_bias[...], proj_w[...], proj_b[...]
    )
    for side, edge in enumerate((left, right)):
        even, odd = edges_out(edge, roll)
        x_tx[side, 0], x_tx[side, 1] = even, odd

    pl.semaphore_wait(barrier, 31)

    mine = lax.div(z, 8)

    def edge_semaphore(side, c):
        return x_recv.at[side * 4 + (1 - side) * 2 * mine + c]

    def edge_copy(side, c, off):
        there = along_z(off)
        return pltpu.make_async_remote_copy(
            src_ref=x_tx.at[side, c, there], dst_ref=x_rx.at[side, c, z], send_sem=x_send,
            recv_sem=edge_semaphore(side, c), device_id=(y_hi * 16 + there, col), device_id_type=MESH,
        )

    for turn in range(4):
        side = (1 - mine) * (turn % 2) + mine * (1 - turn // 2)
        c = (1 - mine) * (turn // 2) + mine * (turn % 2)
        pltpu.make_async_copy(x_tx.at[side, c, z], x_rx.at[side, c, z], edge_semaphore(side, c)).start()
        for off in ORDER:
            edge_copy(side, c, off).start()

    for n in range(5, N_IN):
        fetch[n].wait()
    gate_s[...] = sigmoid(dot_nn(normed, gate_w[...]) + gate_b[...])
    off_s[...] = spread(column(estimate(in_gain[...], in_bias[...], proj_w[...], proj_b[...])), roll)
    wide_s[...] = wide_weight(out_w[...], roll)
    gain_s[...] = spread(column(norm_gain[...]), roll)
    bias_s[...] = spread(column(norm_bias[...]), roll)
    gather_s[...] = gather_const()

    def left_copy(group, c, p):
        return pltpu.make_async_remote_copy(
            src_ref=l_all.at[group, c, chip], dst_ref=l_all.at[group, c, chip], send_sem=l_send,
            recv_sem=l_recv.at[group, c], device_id=(row, p * 2 + core), device_id_type=MESH,
        )

    def other_chips():
        return [
            lax.rem(y_lo + dy, 2) * 4 + lax.rem(x + dx, 4)
            for dx, dy in ((2, 1), (2, 0), (1, 1), (3, 1), (1, 0), (3, 0), (0, 1))
        ]

    def left_out(group, c):
        part = x_rx.at[0, c, pl.ds(8 * group, 8)]
        pltpu.make_async_copy(part, part, x_recv.at[2 * group + c]).wait()
        l_all[group, c, chip] = relay_left(x_rx[0, c, 8 * group : 8 * group + 8].reshape(128, 128))
        for p in other_chips():
            left_copy(group, c, p).start()

    def right_copy(c, s, hi):
        there = (hi * 16 + z, y_hi * 8 + s * 2 + core)
        same = (there[0] == row) & (there[1] == col)
        return same, pltpu.make_async_remote_copy(
            src_ref=r_tx.at[c, s], dst_ref=r_all.at[c, chip], send_sem=r_send, recv_sem=r_recv.at[c],
            device_id=there, device_id_type=MESH,
        )

    def right_out(c):
        part = x_rx.at[1, c]
        pltpu.make_async_copy(part, part, x_recv.at[4 + c]).wait()
        for s in range(4):
            r_tx[c, s] = relay_right(x_rx[1, c, 4 * s : 4 * s + 4].reshape(64, 128))
        for s in range(4):
            for hi in range(2):
                same, copy = right_copy(c, s, hi)

                @pl.when(same)
                def _():
                    pltpu.make_async_copy(r_tx.at[c, s], r_all.at[c, chip], r_recv.at[c]).start()

                @pl.when(jnp.logical_not(same))
                def _():
                    copy.start()

    def sibling_copy(group, c):
        return pltpu.make_async_remote_copy(
            src_ref=t_tx.at[group, c], dst_ref=t_rx.at[group, c], send_sem=t_send, recv_sem=t_recv.at[group, c],
            device_id=sibling, device_id_type=MESH,
        )

    def back_copy(c, there):
        return pltpu.make_async_remote_copy(
            src_ref=u_all.at[there, c], dst_ref=f_rx.at[z, c], send_sem=f_send, recv_sem=f_recv,
            device_id=(y_hi * 16 + there, col), device_id_type=MESH,
        )

    first = core == 0
    operand = [None, None]

    def product(group, c):
        if operand[c] is None:
            part = r_all.at[c]
            pltpu.make_async_copy(part, part, r_recv.at[c]).wait()
            operand[c] = jnp.concatenate(
                [r_all[c, :, 0].reshape(256, 128), r_all[c, :, 1].reshape(256, 128)], axis=1
            )
        part = l_all.at[group, c, pl.ds(0, 7)]
        pltpu.make_async_copy(part, part, l_recv.at[group, c]).wait()
        half = join([l_all[group, c, :, i].reshape(256, 128) for i in range(4)], operand[c], gather_s[...])
        t_tx[group, c] = jnp.where(first, half[:, 128:], half[:, :128])
        t_own[group, c] = jnp.where(first, half[:, :128], half[:, 128:])
        sibling_copy(group, c).start()

    def back(group, c):
        part = t_rx.at[group, c]
        pltpu.make_async_copy(part, part, t_recv.at[group, c]).wait()
        offset = off_s[pl.ds(pl.multiple_of((z * 2 + c) * 16, 16), 16), :]
        total = (t_own[group, c] + t_rx[group, c]).reshape(8, 16, 128) - offset[None]
        u_all[8 * group : 8 * group + 8, c] = total.astype(BF16)

        @pl.loop(8 * group, 8 * group + 8)
        def _(there):
            @pl.when(there == z)
            def _():
                pltpu.make_async_copy(u_all.at[there, c], f_rx.at[there, c], f_recv).start()

            @pl.when(there != z)
            def _():
                back_copy(c, there).start()

    left_out(0, 0)
    right_out(0)
    left_out(0, 1)
    right_out(1)
    left_out(1, 0)
    left_out(1, 1)
    product(0, 0)
    back(0, 0)
    product(0, 1)
    back(0, 1)
    product(1, 0)
    back(1, 0)
    product(1, 1)
    back(1, 1)

    pltpu.make_async_copy(f_rx, f_rx, f_recv).wait()
    values = finish(
        f_rx[...].reshape(512, 128), off_s[...], gain_s[...], bias_s[...], wide_s[...], out_b[...], roll
    )
    for q in range(4):
        update = values[q] * gate_s[q * 128 : (q + 1) * 128]
        out_ref[4 * q : 4 * q + 4] = update.astype(BF16).reshape(4, 32, 128)

    for c in range(2):
        for off in ORDER:
            edge_copy(0, c, off).wait_send()
            edge_copy(1, c, off).wait_send()
            back_copy(c, along_z(off)).wait_send()
        for group in range(2):
            sibling_copy(group, c).wait_send()
            for p in other_chips():
                left_copy(group, c, p).wait_send()
        for s in range(4):
            for hi in range(2):
                same, copy = right_copy(c, s, hi)

                @pl.when(jnp.logical_not(same))
                def _():
                    copy.wait_send()


def per_device(*args):
    args = [a.reshape(1, -1) if a.ndim == 1 else a for a in args]
    dma = pltpu.SemaphoreType.DMA
    return pl.pallas_call(
        kernel,
        out_shape=jax.ShapeDtypeStruct(args[0].shape, BF16),
        in_specs=[pl.BlockSpec(memory_space=pl.ANY)] * N_IN,
        out_specs=pl.BlockSpec(memory_space=pltpu.VMEM),
        scratch_shapes=[pltpu.VMEM(a.shape, a.dtype) for a in args]
        + [
            pltpu.VMEM((2, 2, 16, 16, 128), BF16),
            pltpu.VMEM((2, 2, 16, 16, 128), BF16),
            pltpu.VMEM((2, 2, 8, 4, 32, 128), BF16),
            pltpu.VMEM((2, 4, 2, 32, 128), BF16),
            pltpu.VMEM((2, 8, 2, 32, 128), BF16),
            pltpu.VMEM((2, 2, 128, 128), F32),
            pltpu.VMEM((2, 2, 128, 128), F32),
            pltpu.VMEM((2, 2, 128, 128), F32),
            pltpu.VMEM((16, 2, 16, 128), BF16),
            pltpu.VMEM((16, 2, 16, 128), BF16),
            pltpu.VMEM((512, 128), F32),
            pltpu.VMEM((1024, 256), BF16),
            pltpu.VMEM((512, 512), BF16),
            pltpu.VMEM((512, 128), F32),
            pltpu.VMEM((512, 128), F32),
            pltpu.VMEM((512, 128), F32),
            dma((N_IN,)), dma, dma((6,)), dma, dma((2, 2)), dma, dma((2,)), dma, dma((2, 2)), dma, dma,
        ],
        compiler_params=pltpu.CompilerParams(
            collective_id=0, has_side_effects=True, vmem_limit_bytes=56 * 1024 * 1024
        ),
    )(*args)


def solution(mesh):
    return jax.shard_map(
        per_device,
        mesh=mesh,
        in_specs=(P("row", "col", None), P(), P(), P(), P(), P(), P(), P(), P(), P(), P()),
        out_specs=P("row", "col", None),
        check_vma=False,
    )
```

time: 52.5 us -> 49.2 us (0.937)
  Pallas kernels: 50.2 us -> 47.4 us
    pallas_call x1, Pallas kernels: 50.2 us -> 47.4 us  [per_device(): pl.pallas_call(kernel, out_shape=jax.ShapeDtypeStruct(args[0].shape, BF16...]
where the time goes in v3:
time: 49.2 us; the launch traced here: 49 us
  Pallas kernels  47.4 us (96%)
  local copies, waits for them, and re-layouts  1.57 us (3%)
    pallas_call x1, Pallas kernels, per_device(): pl.pallas_call(kernel, out_shape=jax.ShapeDtypeStruct(args[0].shape, BF16...  47.4 us
    unnamed x1, local copies, waits for them, and re-layouts  1.57 us

profile of v3, /device:TPU:1, one launch (start us, length us, event | category | flops | bytes accessed | tf_op | source)
XLA Modules:
  0.0 49.0 jit_solution(16088404358297769843)
XLA Ops:
  0.0 47.4 %shard_map.109 = bf16[16,32,128]{2,1,0:T(8,128)(2,1)} custom-call(bf16[16,32,128]{2,1,0:T(8,128)(2,1)} %refs_0_.1, f32[1,128]{1,0:T(1,128)} %bitcast.8, f32[1,128]{1,0:T(1,128)} %bitcast.9, bf16[128,512]{1,0:T(8,128)(2,1)} %refs_3_.1, f32[1,512]{1,0:T(1,128)} %bitcast.7, f32[1,128]{1,0:T(1,128)} %bitcast.10, f32[1,128]{1,0:T(1,128)} %bitcast.11, ...), custom_call_target="tpu_custom_call" | custom-call | tf_op jit(solution)/shard_map/pallas_call | solution.py:354
  47.4 1.6 %copy.13 = bf16[16,32,128]{2,1,0:T(8,128)(2,1)} copy(bf16[16,32,128]{2,1,0:T(8,128)(2,1)} %shard_map.109) | data formatting | bytes 262144

commit v4 on v3

--- a/solution.py
+++ b/solution.py
@@ -154,10 +154,6 @@
         in_sem, x_send, x_recv, l_send, l_recv, r_send, r_recv, t_send, t_recv, f_send, f_recv,
     ) = rest
     roll = pltpu.roll
-    fetch = [pltpu.make_async_copy(hbm[n], held[n], in_sem.at[n]) for n in range(N_IN)]
-    for copy in fetch:
-        copy.start()
-
     row, col = lax.axis_index("row"), lax.axis_index("col")
     y_hi, z = lax.div(row, 16), lax.rem(row, 16)
     y_lo, x, core = lax.div(col, 8), lax.rem(lax.div(col, 2), 4), lax.rem(col, 2)
@@ -172,6 +168,9 @@
 
     for off in ORDER:
         greet((y_hi * 16 + along_z(off), col))
+    fetch = [pltpu.make_async_copy(hbm[n], held[n], in_sem.at[n]) for n in range(N_IN)]
+    for copy in fetch:
+        copy.start()
     for t in range(1, 16):
         p = lax.rem(y_hi * 8 + chip + t, 16)
         greet((lax.div(p, 8) * 16 + z, lax.rem(p, 8) * 2 + core))
@@ -202,8 +201,8 @@
         )
 
     for turn in range(4):
-        side = (1 - mine) * (turn % 2) + mine * (1 - turn // 2)
-        c = (1 - mine) * (turn // 2) + mine * (turn % 2)
+        side = (1 - mine) * (0, 0, 1, 1)[turn] + mine * (1, 1, 0, 0)[turn]
+        c = (1 - mine) * (0, 1, 0, 1)[turn] + mine * (0, 1, 0, 1)[turn]
         pltpu.make_async_copy(x_tx.at[side, c, z], x_rx.at[side, c, z], edge_semaphore(side, c)).start()
         for off in ORDER:
             edge_copy(side, c, off).start()
@@ -308,8 +307,8 @@
                 back_copy(c, there).start()
 
     left_out(0, 0)
+    left_out(0, 1)
     right_out(0)
-    left_out(0, 1)
     right_out(1)
     left_out(1, 0)
     left_out(1, 1)
@@ -322,6 +321,20 @@
     product(1, 1)
     back(1, 1)
 
+    def left_here(part, semaphore):
+        pltpu.make_async_copy(part, part, semaphore).wait()
+
+    left_here(x_tx.at[:, :, pl.ds(0, 15)], x_send)
+    left_here(l_all.at[:, :, pl.ds(0, 7)], l_send)
+    left_here(r_all.at[:, pl.ds(0, 7)], r_send)
+
+    @pl.when(y_lo != y_hi)
+    def _():
+        left_here(r_all.at[:, pl.ds(0, 1)], r_send)
+
+    left_here(t_tx, t_send)
+    left_here(f_rx.at[pl.ds(0, 15)], f_send)
+
     pltpu.make_async_copy(f_rx, f_rx, f_recv).wait()
     values = finish(
         f_rx[...].reshape(512, 128), off_s[...], gain_s[...], bias_s[...], wide_s[...], out_b[...], roll
@@ -329,23 +342,6 @@
     for q in range(4):
         update = values[q] * gate_s[q * 128 : (q + 1) * 128]
         out_ref[4 * q : 4 * q + 4] = update.astype(BF16).reshape(4, 32, 128)
-
-    for c in range(2):
-        for off in ORDER:
-            edge_copy(0, c, off).wait_send()
-            edge_copy(1, c, off).wait_send()
-            back_copy(c, along_z(off)).wait_send()
-        for group in range(2):
-            sibling_copy(group, c).wait_send()
-            for p in other_chips():
-                left_copy(group, c, p).wait_send()
-        for s in range(4):
-            for hi in range(2):
-                same, copy = right_copy(c, s, hi)
-
-                @pl.when(jnp.logical_not(same))
-                def _():
-                    copy.wait_send()
 
 
 def per_device(*args):
@@ -377,9 +373,9 @@
             dma((N_IN,)), dma, dma((6,)), dma, dma((2, 2)), dma, dma((2,)), dma, dma((2, 2)), dma, dma,
         ],
         compiler_params=pltpu.CompilerParams(
-            collective_id=0, has_side_effects=True, vmem_limit_bytes=56 * 1024 * 1024
+            collective_id=0, has_side_effects=True, vmem_limit_bytes=40 * 1024 * 1024
         ),
-    )(*args)
+    )(*[pltpu.with_memory_space_constraint(a, pltpu.HBM) for a in args])
 
 
 def solution(mesh):

time: 49.2 us -> 47.2 us (0.959)
  Pallas kernels: 47.4 us -> 46.2 us
  local copies, waits for them, and re-layouts: 1.57 us -> 0.66 us
    pallas_call x1, Pallas kernels: 47.4 us -> 46.2 us  [per_device(): pl.pallas_call(kernel, out_shape=jax.ShapeDtypeStruct(args[0].shape, BF16...]
    unnamed x1, local copies, waits for them, and re-layouts: 1.57 us -> 0.66 us
where the time goes in v4:
time: 47.2 us; the launch traced here: 46.8 us
  Pallas kernels  46.2 us (98%)
  local copies, waits for them, and re-layouts  0.66 us (1%)
    pallas_call x1, Pallas kernels, per_device(): pl.pallas_call(kernel, out_shape=jax.ShapeDtypeStruct(args[0].shape, BF16...  46.2 us

profile of v4, /device:TPU:1, one launch (start us, length us, event | category | flops | bytes accessed | tf_op | source)
XLA Modules:
  0.0 46.8 jit_solution(3097803486884792573)
XLA Ops:
  0.0 46.2 %shard_map.109 = bf16[16,32,128]{2,1,0:T(8,128)(2,1)S(1)} custom-call(bf16[16,32,128]{2,1,0:T(8,128)(2,1)} %refs_0_.1, f32[1,128]{1,0:T(1,128)} %bitcast.8, f32[1,128]{1,0:T(1,128)} %bitcast.9, bf16[128,512]{1,0:T(8,128)(2,1)} %refs_3_.1, f32[1,512]{1,0:T(1,128)} %bitcast.7, f32[1,128]{1,0:T(1,128)} %bitcast.10, f32[1,128]{1,0:T(1,128)} %bitcast.11, ...), custom_call_target="tpu_custom_call" | custom-call | tf_op jit(solution)/shard_map/pallas_call | solution.py:350
  46.2 0.7 %copy.13 = bf16[16,32,128]{2,1,0:T(8,128)(2,1)} copy(bf16[16,32,128]{2,1,0:T(8,128)(2,1)S(1)} %shard_map.109) | data formatting | bytes 262144

commit v5 on v4

--- a/solution.py
+++ b/solution.py
@@ -65,11 +65,15 @@
 
 
 def relay_right(rows):
-    twice = jnp.concatenate([rows, rows], axis=0)
-    r, c = iota((64, 128), 0), iota((64, 128), 1)
-    base = (r // 32) * 64 + r % 32
-    halves = [dot_nt(jnp.where(c == base + 32 * p, 1.0, 0.0).astype(BF16), twice) for p in range(2)]
-    return jnp.where(c < 64, halves[0], halves[1]).astype(BF16).reshape(2, 32, 128)
+    turned = dot_nt(eye(128), rows)
+    low = iota((32, 128), 1) < 64
+    out = []
+    for s in range(4):
+        pair = turned[:, 128 * (s // 2) : 128 * (s // 2) + 128].reshape(4, 32, 128)
+        swapped = [pltpu.roll(pair[j], 64, 1) for j in range(4)]
+        first, second = (pair, swapped) if s % 2 == 0 else (swapped, pair)
+        out.append([jnp.where(low, first[2 * t], second[2 * t + 1]).astype(BF16) for t in range(2)])
+    return out
 
 
 def gather_const():
@@ -137,8 +141,7 @@
     var = group_sum(jnp.sum(centred * centred, axis=0), roll) * (1.0 / 128)
     scale = lax.rsqrt(var + 1e-05)
     normed = (centred * scale[None]).reshape(512, 128) * gain + bias
-    turned = dot_nt(eye(128), normed.astype(BF16)).astype(BF16)
-    value = dot_nn(turned, wide)
+    value = lax.dot_general(normed.astype(BF16), wide, (((0,), (0,)), ((), ())), preferred_element_type=F32)
     return [value[:, q * 128 : (q + 1) * 128] + out_b for q in range(4)]
 
 
@@ -201,8 +204,8 @@
         )
 
     for turn in range(4):
-        side = (1 - mine) * (0, 0, 1, 1)[turn] + mine * (1, 1, 0, 0)[turn]
-        c = (1 - mine) * (0, 1, 0, 1)[turn] + mine * (0, 1, 0, 1)[turn]
+        side = (1 - mine) * (0, 0, 1, 1)[turn] + mine * (1, 0, 1, 0)[turn]
+        c = (1 - mine) * (0, 1, 0, 1)[turn] + mine * (0, 0, 1, 1)[turn]
         pltpu.make_async_copy(x_tx.at[side, c, z], x_rx.at[side, c, z], edge_semaphore(side, c)).start()
         for off in ORDER:
             edge_copy(side, c, off).start()
@@ -246,8 +249,9 @@
     def right_out(c):
         part = x_rx.at[1, c]
         pltpu.make_async_copy(part, part, x_recv.at[4 + c]).wait()
+        blocks = relay_right(x_rx[1, c].reshape(256, 128))
         for s in range(4):
-            r_tx[c, s] = relay_right(x_rx[1, c, 4 * s : 4 * s + 4].reshape(64, 128))
+            r_tx[c, s, 0], r_tx[c, s, 1] = blocks[s]
         for s in range(4):
             for hi in range(2):
                 same, copy = right_copy(c, s, hi)

time: 47.2 us -> 47.1 us (level)
  no operation moved by 1% of the time
where the time goes in v5:
time: 47.1 us; the launch traced here: 46.7 us
  Pallas kernels  46 us (98%)
  local copies, waits for them, and re-layouts  0.66 us (1%)
    pallas_call x1, Pallas kernels, per_device(): pl.pallas_call(kernel, out_shape=jax.ShapeDtypeStruct(args[0].shape, BF16...  46 us

profile of v5, /device:TPU:1, one launch (start us, length us, event | category | flops | bytes accessed | tf_op | source)
XLA Modules:
  0.0 46.7 jit_solution(915484055241261227)
XLA Ops:
  0.0 46.0 %shard_map.109 = bf16[16,32,128]{2,1,0:T(8,128)(2,1)S(1)} custom-call(bf16[16,32,128]{2,1,0:T(8,128)(2,1)} %refs_0_.1, f32[1,128]{1,0:T(1,128)} %bitcast.8, f32[1,128]{1,0:T(1,128)} %bitcast.9, bf16[128,512]{1,0:T(8,128)(2,1)} %refs_3_.1, f32[1,512]{1,0:T(1,128)} %bitcast.7, f32[1,128]{1,0:T(1,128)} %bitcast.10, f32[1,128]{1,0:T(1,128)} %bitcast.11, ...), custom_call_target="tpu_custom_call" | custom-call | tf_op jit(solution)/shard_map/pallas_call | solution.py:354
  46.1 0.7 %copy.13 = bf16[16,32,128]{2,1,0:T(8,128)(2,1)} copy(bf16[16,32,128]{2,1,0:T(8,128)(2,1)S(1)} %shard_map.109) | data formatting | bytes 262144

commit v6 on v5

--- a/solution.py
+++ b/solution.py
@@ -174,9 +174,14 @@
     fetch = [pltpu.make_async_copy(hbm[n], held[n], in_sem.at[n]) for n in range(N_IN)]
     for copy in fetch:
         copy.start()
-    for t in range(1, 16):
-        p = lax.rem(y_hi * 8 + chip + t, 16)
-        greet((lax.div(p, 8) * 16 + z, lax.rem(p, 8) * 2 + core))
+    for t in range(1, 8):
+        greet((row, lax.rem(chip + t, 8) * 2 + core))
+
+    @pl.when(y_lo != y_hi)
+    def _():
+        for p in range(8):
+            greet(((1 - y_hi) * 16 + z, p * 2 + core))
+
     sibling = (row, col + 1 - 2 * core)
     greet(sibling)
 
@@ -189,7 +194,7 @@
         even, odd = edges_out(edge, roll)
         x_tx[side, 0], x_tx[side, 1] = even, odd
 
-    pl.semaphore_wait(barrier, 31)
+    pl.semaphore_wait(barrier, 27)
 
     mine = lax.div(z, 8)
 

time: 47.1 us -> 47.2 us (level)
  no operation moved by 1% of the time
where the time goes in v6:
time: 47.2 us; the launch traced here: 47.1 us
  Pallas kernels  46.4 us (98%)
  local copies, waits for them, and re-layouts  0.66 us (1%)
    pallas_call x1, Pallas kernels, per_device(): pl.pallas_call(kernel, out_shape=jax.ShapeDtypeStruct(args[0].shape, BF16...  46.4 us

profile of v6, /device:TPU:1, one launch (start us, length us, event | category | flops | bytes accessed | tf_op | source)
XLA Modules:
  0.0 47.1 jit_solution(1394165649088014430)
XLA Ops:
  0.0 46.4 %shard_map.109 = bf16[16,32,128]{2,1,0:T(8,128)(2,1)S(1)} custom-call(bf16[16,32,128]{2,1,0:T(8,128)(2,1)} %refs_0_.1, f32[1,128]{1,0:T(1,128)} %bitcast.8, f32[1,128]{1,0:T(1,128)} %bitcast.9, bf16[128,512]{1,0:T(8,128)(2,1)} %refs_3_.1, f32[1,512]{1,0:T(1,128)} %bitcast.7, f32[1,128]{1,0:T(1,128)} %bitcast.10, f32[1,128]{1,0:T(1,128)} %bitcast.11, ...), custom_call_target="tpu_custom_call" | custom-call | tf_op jit(solution)/shard_map/pallas_call | solution.py:359
  46.4 0.7 %copy.13 = bf16[16,32,128]{2,1,0:T(8,128)(2,1)} copy(bf16[16,32,128]{2,1,0:T(8,128)(2,1)S(1)} %shard_map.109) | data formatting | bytes 262144
